TPU v7x, 256 devices: a whole 4x4x8 slice. The times are simulated.
256 devices in a mesh: row: 4 (over x), tm: 64 (over z, y, core).
Axes of the slice: x: 4, y: 4, z: 8, core: 2. Of those that a mesh axis runs over, the one named last changes fastest.
Arguments:
- snapshots: bfloat16 [64, 2048, 2048], P('tm', 'row'), may hold values from -10 to 10
- basis: bfloat16 [64, 2048, 64], P('tm', 'row'), may hold values from -0.125 to 0.125
- neighbour_ids: int32 [64, 2], replicated, may hold values from 0 to 63, as said below
Outputs:
- feature_gram: float32 [64, 2272, 2272], P('tm', 'row')
Inputs may be any that keep to these rules, and one draw needn't show every extreme that they name: `neighbour_ids`: row s is coupled to subdomain s - 1 (cyclically, around the annulus) in its first entry, and in its second to another subdomain that is neither s nor s - 1.
All inputs are finite; a program needn't handle non-finite values.
Results may differ from a plain program's by a relative error of at most 0.005.
Values may be sent and summed in bfloat16 or wider, within the bound.
A program may use at most 64 MiB of HBM per device.

v0:
```python
import jax
import jax.numpy as jnp
import numpy as np
from jax import lax
from jax.sharding import PartitionSpec as P


def pair_tables(rank):
    upper_i, upper_j = np.triu_indices(rank)
    lines = np.arange(rank)[:, None]
    left_table = jnp.asarray((lines == upper_i[None, :]).astype(np.float32), dtype=jnp.bfloat16)
    right_table = jnp.asarray((lines == upper_j[None, :]).astype(np.float32), dtype=jnp.bfloat16)
    return (left_table, right_table)


def on_device(snapshots, basis, neighbour_ids):
    shard = snapshots[0]
    columns = basis[0]
    rank = columns.shape[1]
    coupled = neighbour_ids.shape[1]
    row_count = lax.axis_size("row")
    total_time = shard.shape[1]
    row_pos = lax.axis_index("row")
    block = shard
    local = lax.psum_scatter(
        lax.dot_general(
            block, columns, (((0,), (0,)), ((), ())), preferred_element_type=jnp.float32
        ),
        "row",
        scatter_dimension=0,
        tiled=True,
    )
    energy = lax.psum(jnp.sum(local * local, axis=0), "row")
    scale = lax.rsqrt(energy / total_time + 1e-06)
    normed = (local * scale).astype(jnp.bfloat16)
    every = lax.all_gather(normed[None], "tm", axis=0, tiled=True)
    subdomains = every.shape[0]
    own_index = lax.axis_index("tm")
    listed = lax.dynamic_slice_in_dim(neighbour_ids, own_index, 1, 0)[0]
    picker = (listed[:, None] == jnp.arange(subdomains, dtype=jnp.int32)[None, :]).astype(
        jnp.bfloat16
    )
    chosen = jnp.einsum("ks,str->ktr", picker, every, preferred_element_type=jnp.float32).astype(
        jnp.bfloat16
    )
    stacked = jnp.concatenate([normed[None], chosen], axis=0)
    k_total = rank * (1 + coupled) + rank * (rank + 1) // 2
    row_block = k_total // row_count
    left_table, right_table = pair_tables(rank)

    def features(block):
        own = block[0]
        left = jnp.dot(own, left_table, preferred_element_type=jnp.float32)
        right = jnp.dot(own, right_table, preferred_element_type=jnp.float32)
        quad = (left * right).astype(jnp.bfloat16)
        return jnp.concatenate([block[slot] for slot in range(block.shape[0])] + [quad], axis=1)

    def add_block(total, block):
        feats = features(block)
        rows = lax.dynamic_slice_in_dim(feats, row_pos * row_block, row_block, 1)
        return total + lax.dot_general(
            rows, feats, (((0,), (0,)), ((), ())), preferred_element_type=jnp.float32
        )

    initial = jnp.zeros((row_block, k_total), jnp.float32)
    carry = initial
    piece = lax.all_gather(stacked, "row", axis=1, tiled=True)
    length = piece.shape[1]
    blocks = jnp.moveaxis(piece.reshape(piece.shape[0], length // 512, 512, rank), 1, 0)

    def step_block(total, block):
        return (add_block(total, block), None)

    carry, unused = lax.scan(step_block, carry, blocks)
    return (carry / total_time)[None]


def solution(mesh):
    return jax.shard_map(
        on_device,
        mesh=mesh,
        in_specs=(P("tm", "row", None), P("tm", "row", None), P()),
        out_specs=P("tm", "row", None),
        check_vma=False,
    )
```

profile of v0, /device:TPU:1, one launch (start us, length us, event | category | flops | bytes accessed | tf_op | source)
XLA Modules:
  0.0 190.6 jit_solution(2646163556897279114)
XLA Ops:
  6.5 1.6 copy-done
  8.1 2.1 %fusion.3 = f32[2048,64]{0,1:T(8,128)} fusion(bf16[1,512,2048]{2,1,0:T(8,128)(2,1)S(1)} %copy-done, bf16[1,512,64]{1,2,0:T(8,128)(2,1)} %param.8), kind=kOutput, calls=%fused_computation.10 | convolution fusion | flops 134217728 | bytes 2686976 | tf_op jit(solution)/shard_map/dot_general | solution.py:26
  10.3 26.2 %reduce-scatter.2.cloned.1.call-done = f32[512,64]{0,1:T(8,128)} async-done(((f32[2048,64]{0,1:T(8,128)}), f32[512,64]{0,1:T(8,128)}) %reduce-scatter.2.cloned.1.call-update) | async-done | bytes 131088 | tf_op jit(solution)/shard_map/reduce_scatter | solution.py:25
  36.5 1.0 multiply_reduce_fusion
  37.5 6.6 %psum.7 = f32[64]{0:T(128)S(1)} all-reduce(f32[64]{0:T(128)S(1)} %multiply_reduce_fusion), channel_id=1, replica_groups=mesh['row'=4,'tm'=64] {'row'}, use_global_device_ids=true, to_apply=%region_2.0 | all-reduce | flops 64 | bytes 512 | tf_op jit(solution)/shard_map/psum | solution.py:33
  44.1 1.6 multiply_convert_fusion
  45.8 0.9 dynamic-slice_reduce_fusion
  46.6 1.0 fusion.17
  47.7 78.1 %all-gather.3.cloned.1.call-done = bf16[32768,64]{0,1:T(8,128)(2,1)} async-done(((bf16[512,64]{0,1:T(8,128)(2,1)}), bf16[32768,64]{0,1:T(8,128)(2,1)}) %all-gather.3.cloned.1.call-update) | async-done | bytes 4194320 | tf_op jit(solution)/shard_map/all_gather | solution.py:36
  125.8 3.8 %copy.13 = bf16[8,8,64,512]{3,2,1,0:T(8,128)(2,1)S(1)} copy(bf16[8,8,64,512]{3,1,2,0:T(8,128)(2,1)} %bitcast.48) | data formatting | bytes 8388608
  130.6 13.4 %all_gather.7 = bf16[3,2048,64]{1,0,2:T(4,128)(2,1)} all-gather(bf16[3,512,64]{1,0,2:T(4,128)(2,1)S(1)} %pad_maximum_fusion.1), channel_id=1, replica_groups=mesh['row'=4,'tm'=64] {'row'}, dimensions={1}, use_global_device_ids=true | all-gather | bytes 983040 | tf_op jit(solution)/shard_map/all_gather | solution.py:67
  144.1 3.6 %reshape.14 = bf16[3,4,512,64]{2,1,0,3:T(4,128)(2,1)} reshape(bf16[3,2048,64]{1,0,2:T(4,128)(2,1)} %all_gather.7) | data formatting | bytes 1572864 | tf_op jit(solution)/shard_map/reshape | solution.py:69
  147.6 1.3 copy.10
  148.9 29.6 %while.14 = (s32[]{:T(128)}, f32[568,2272]{1,0:T(8,128)}, bf16[4,3,512,64]{2,3,1,0:T(8,128)(2,1)S(1)}, s32[]{:T(128)}, s32[]{:T(128)}, /*index=5*/s32[]{:T(128)}...) while((s32[]{:T(128)}, f32[568,2272]{1,0:T(8,128)}, ...), condition=%wide.region_4.5_spmd.clone.clone, body=%wide.region_3.4_spmd.sunk.clone.clone.sunk | while | flops 1608114688 | bytes 66016488 | solution.py:74
  149.8 0.8 fusion.33
  151.7 2.3 %convolution_add_fusion.2 = f32[568,2272]{1,0:T(8,128)S(1)} fusion(bf16[512,2272]{0,1:T(8,128)(2,1)S(1)} %pad_maximum_fusion.3, f32[568,2272]{1,0:T(8,128)S(1)} %bitcast.46, pred[]{:T(512)S(6)} %compare.3, s32[]{:T(128)} %get-tuple-element.182), kind=kOutput, calls=%fused_computation.clone.1 | convolution fusion | flops 1324048896 | bytes 13304837 | tf_op jit(solution)/shard_map/while/body/eval_jaxpr/dot_general | solution.py:61
  154.0 2.3 %copy-done.1 = f32[568,2272]{1,0:T(8,128)} copy-done((f32[568,2272]{1,0:T(8,128)}, f32[568,2272]{1,0:T(8,128)S(1)}, u32[]{:S(2)}) %copy-start.1) | copy-done | bytes 5162008 | tf_op jit(solution)/shard_map/while
  159.1 2.3 %convolution_add_fusion.2 = f32[568,2272]{1,0:T(8,128)S(1)} fusion(bf16[512,2272]{0,1:T(8,128)(2,1)S(1)} %pad_maximum_fusion.3, f32[568,2272]{1,0:T(8,128)S(1)} %bitcast.46, pred[]{:T(512)S(6)} %compare.3, s32[]{:T(128)} %get-tuple-element.182), kind=kOutput, calls=%fused_computation.clone.1 | convolution fusion | flops 1324048896 | bytes 13304837 | tf_op jit(solution)/shard_map/while/body/eval_jaxpr/dot_general | solution.py:61
  161.4 2.3 %copy-done.1 = f32[568,2272]{1,0:T(8,128)} copy-done((f32[568,2272]{1,0:T(8,128)}, f32[568,2272]{1,0:T(8,128)S(1)}, u32[]{:S(2)}) %copy-start.1) | copy-done | bytes 5162008 | tf_op jit(solution)/shard_map/while
  166.5 2.3 %convolution_add_fusion.2 = f32[568,2272]{1,0:T(8,128)S(1)} fusion(bf16[512,2272]{0,1:T(8,128)(2,1)S(1)} %pad_maximum_fusion.3, f32[568,2272]{1,0:T(8,128)S(1)} %bitcast.46, pred[]{:T(512)S(6)} %compare.3, s32[]{:T(128)} %get-tuple-element.182), kind=kOutput, calls=%fused_computation.clone.1 | convolution fusion | flops 1324048896 | bytes 13304837 | tf_op jit(solution)/shard_map/while/body/eval_jaxpr/dot_general | solution.py:61
  168.8 2.3 %copy-done.1 = f32[568,2272]{1,0:T(8,128)} copy-done((f32[568,2272]{1,0:T(8,128)}, f32[568,2272]{1,0:T(8,128)S(1)}, u32[]{:S(2)}) %copy-start.1) | copy-done | bytes 5162008 | tf_op jit(solution)/shard_map/while
  173.9 2.3 %convolution_add_fusion.2 = f32[568,2272]{1,0:T(8,128)S(1)} fusion(bf16[512,2272]{0,1:T(8,128)(2,1)S(1)} %pad_maximum_fusion.3, f32[568,2272]{1,0:T(8,128)S(1)} %bitcast.46, pred[]{:T(512)S(6)} %compare.3, s32[]{:T(128)} %get-tuple-element.182), kind=kOutput, calls=%fused_computation.clone.1 | convolution fusion | flops 1324048896 | bytes 13304837 | tf_op jit(solution)/shard_map/while/body/eval_jaxpr/dot_general | solution.py:61
  176.2 2.3 %copy-done.1 = f32[568,2272]{1,0:T(8,128)} copy-done((f32[568,2272]{1,0:T(8,128)}, f32[568,2272]{1,0:T(8,128)S(1)}, u32[]{:S(2)}) %copy-start.1) | copy-done | bytes 5162008 | tf_op jit(solution)/shard_map/while
  178.6 5.2 %multiply_bitcast_fusion = f32[1,568,2272]{2,1,0:T(8,128)} fusion(f32[568,2272]{1,0:T(8,128)} %get-tuple-element.80), kind=kLoop, calls=%fused_computation.9 | loop fusion | flops 1290496 | bytes 10323968 | tf_op jit(solution)/shard_map/broadcast_in_dim | solution.py:75
  (53 shorter events, 11.1 us)
Async XLA Ops:
  6.5 1.6 copy-start
  6.5 30.0 %reduce-scatter.2.cloned.1.call-start = ((), (), s32[]{:S(2)}) async-start(), calls=%async_computation.1 | async-start | bytes 655360 | tf_op jit(solution)/shard_map/reduce_scatter | solution.py:25
  10.3 115.6 %all-gather.3.cloned.1.call-start = ((), (), s32[]{:S(2)}) async-start(), calls=%async_computation.2 | async-start | bytes 4259840 | tf_op jit(solution)/shard_map/all_gather | solution.py:36
  129.6 19.3 %copy-start.2 = (bf16[64,2080]{1,0:T(8,128)(2,1)S(1)}, bf16[64,2080]{1,0:T(8,128)(2,1)}, u32[]{:S(2)}) copy-start(bf16[64,2080]{1,0:T(8,128)(2,1)} %constant.52.clone..sunk.3) | copy-start | bytes 798724
  129.6 19.3 %copy-start.3 = (bf16[64,2080]{1,0:T(8,128)(2,1)S(1)}, bf16[64,2080]{1,0:T(8,128)(2,1)}, u32[]{:S(2)}) copy-start(bf16[64,2080]{1,0:T(8,128)(2,1)} %constant.51.clone..sunk.3) | copy-start | bytes 798724
  149.0 2.2 %slice-start = ((s8[5234688]{0:T(1024)(128)(4,1)}), s8[4194304]{0:T(1024)(128)(4,1)S(1)}, s32[]{:S(2)}) async-start(s8[5234688]{0:T(1024)(128)(4,1)} %bitcast.45), calls=%async_computation.3 | async-start | bytes 8388608 | tf_op jit(solution)/shard_map/while
  149.8 1.9 slice-start.1
  154.0 2.4 %copy-start.1 = (f32[568,2272]{1,0:T(8,128)}, f32[568,2272]{1,0:T(8,128)S(1)}, u32[]{:S(2)}) copy-start(f32[568,2272]{1,0:T(8,128)S(1)} %convolution_add_fusion.2) | copy-start | bytes 15485956 | tf_op jit(solution)/shard_map/while
  156.4 2.2 %slice-start = ((s8[5234688]{0:T(1024)(128)(4,1)}), s8[4194304]{0:T(1024)(128)(4,1)S(1)}, s32[]{:S(2)}) async-start(s8[5234688]{0:T(1024)(128)(4,1)} %bitcast.45), calls=%async_computation.3 | async-start | bytes 8388608 | tf_op jit(solution)/shard_map/while
  157.2 1.9 slice-start.1
  161.4 2.4 %copy-start.1 = (f32[568,2272]{1,0:T(8,128)}, f32[568,2272]{1,0:T(8,128)S(1)}, u32[]{:S(2)}) copy-start(f32[568,2272]{1,0:T(8,128)S(1)} %convolution_add_fusion.2) | copy-start | bytes 15485956 | tf_op jit(solution)/shard_map/while
  163.8 2.2 %slice-start = ((s8[5234688]{0:T(1024)(128)(4,1)}), s8[4194304]{0:T(1024)(128)(4,1)S(1)}, s32[]{:S(2)}) async-start(s8[5234688]{0:T(1024)(128)(4,1)} %bitcast.45), calls=%async_computation.3 | async-start | bytes 8388608 | tf_op jit(solution)/shard_map/while
  164.6 1.9 slice-start.1
  168.8 2.4 %copy-start.1 = (f32[568,2272]{1,0:T(8,128)}, f32[568,2272]{1,0:T(8,128)S(1)}, u32[]{:S(2)}) copy-start(f32[568,2272]{1,0:T(8,128)S(1)} %convolution_add_fusion.2) | copy-start | bytes 15485956 | tf_op jit(solution)/shard_map/while
  171.2 2.2 %slice-start = ((s8[5234688]{0:T(1024)(128)(4,1)}), s8[4194304]{0:T(1024)(128)(4,1)S(1)}, s32[]{:S(2)}) async-start(s8[5234688]{0:T(1024)(128)(4,1)} %bitcast.45), calls=%async_computation.3 | async-start | bytes 8388608 | tf_op jit(solution)/shard_map/while
  172.0 1.9 slice-start.1
  176.2 2.4 %copy-start.1 = (f32[568,2272]{1,0:T(8,128)}, f32[568,2272]{1,0:T(8,128)S(1)}, u32[]{:S(2)}) copy-start(f32[568,2272]{1,0:T(8,128)S(1)} %convolution_add_fusion.2) | copy-start | bytes 15485956 | tf_op jit(solution)/shard_map/while
Sparse Core Ops, SparseCore 0:
  10.4 26.0 reduce-scatter.1
  45.9 79.9 all-gather.2
where the time goes:
time: 193 us; the launch traced here: 191 us
  waiting for transfers between devices  104 us (54%)
  local copies, waits for them, and re-layouts  24.5 us (13%)
  blocking collectives  20 us (10%)
  matrix products  18.3 us (9%)
  between operations  13.5 us (7%)
  other arithmetic  9.68 us (5%)
    all_gather x1, waiting for transfers between devices, on_device(): every = lax.all_gather(normed[None], 'tm', axis=0, tiled=True)  78.1 us
    reduce_scatter x1, waiting for transfers between devices, on_device(): lax.psum_scatter(lax.dot_general(block, columns, (((0,), (0,)), ((), ()))...  26.2 us
    all_gather x1, blocking collectives, on_device(): piece = lax.all_gather(stacked, 'row', axis=1, tiled=True)  13.4 us
    while x24, local copies, waits for them, and re-layouts  13.3 us
    dot_general x4, matrix products, add_block(): lax.dot_general(rows, feats, (((0,), (0,)), ((), ())), preferred_element_...  9.34 us
    unnamed x8, local copies, waits for them, and re-layouts  6.66 us
    psum x1, blocking collectives, on_device(): energy = lax.psum(jnp.sum(local * local, axis=0), 'row')  6.59 us
    broadcast_in_dim x1, other arithmetic, on_device(): return (carry / total_time)[None]  5.18 us
  transfers between devices with their start and end apart: 2, of which 2 were waited for; matrix products, arithmetic and copies ran while one was open for 1% of the time, Pallas kernels for 0%

commit v1 on v0

v1 whole, which is shorter than its diff:
```python
import jax
import jax.numpy as jnp
import numpy as np
from jax import lax
from jax.experimental import pallas as pl
from jax.experimental.pallas import tpu as pltpu
from jax.sharding import PartitionSpec as P

MESH = pl.DeviceIdType.MESH
BF = jnp.bfloat16
F32 = jnp.float32


def place():
    t = lax.axis_index("tm")
    return lax.axis_index("row"), lax.div(t, 8), lax.rem(lax.div(t, 2), 4), lax.rem(t, 2)


def at(x, z, y, c):
    return (lax.rem(x, 4), (lax.rem(z, 8) * 4 + lax.rem(y, 4)) * 2 + lax.rem(c, 2))


def comm_kernel(snap, basis, ids, own, n1, n2, sv, psend, precv, gath, zsend, zrecv,
                ld, ps, pr, os, orr, ys, yr, cs, cr, ns, nr, n1s, n1r, zs, zr, n2s, n2r):
    x, z, y, c = place()
    s = lax.axis_index("tm")
    s_next = (lax.axis_index("row"), lax.rem(s + 1, 64))
    s_prev = (lax.axis_index("row"), lax.rem(s + 63, 64))

    def cols(q):
        return pl.ds(pl.multiple_of(q * 512, 512), 512)

    def remote(src, dst, ss, rs, dev):
        return pltpu.make_async_remote_copy(src_ref=src, dst_ref=dst, send_sem=ss, recv_sem=rs,
                                            device_id=dev, device_id_type=MESH)

    quarter = [lax.rem(x + k, 4) for k in (1, 2, 3, 0)]
    loads = [pltpu.make_async_copy(snap.at[:, cols(q)], sv.at[:, cols(q)], ld.at[i]) for i, q in enumerate(quarter)]
    for cp in loads:
        cp.start()

    bar = pltpu.get_barrier_semaphore()
    peers = [at(x + k, z, y, c) for k in (1, 2, 3)] + [at(x, z, y + k, c) for k in (1, 2, 3)]
    peers += [at(x, z + k, y, c) for k in range(1, 8)] + [at(x, z, y, c + 1), s_next, s_prev]
    for p in peers:
        pl.semaphore_signal(bar, inc=1, device_id=p, device_id_type=MESH)

    def project(i):
        loads[i].wait()
        return lax.dot_general(basis[...], sv[:, cols(quarter[i])], (((0,), (0,)), ((), ())), preferred_element_type=F32)

    sums = []
    for i in range(3):
        psend[i] = project(i).astype(BF)
        if i == 0:
            pl.semaphore_wait(bar, len(peers))
        cp = remote(psend.at[i], precv.at[i], ps.at[i], pr.at[i], at(x + i + 1, z, y, c))
        cp.start()
        sums.append(cp)
    total = project(3)
    for i in range(3):
        sums[i].wait_recv()
        total = total + precv[i].astype(F32)

    me = y * 2 + c
    gath[me] = total.astype(BF)
    own[x] = total
    ycp, ccp = [], []
    for k in (1, 2, 3):
        cp = remote(gath.at[me], gath.at[me], ys.at[k - 1], yr.at[k - 1], at(x, z, y + k, c))
        cp.start()
        ycp.append(cp)
    cp = remote(gath.at[me], gath.at[me], cs.at[0], cr.at[0], at(x, z, y, c + 1))
    cp.start()
    ccp.append(cp)
    ncp = remote(gath.at[me], n1.at[x], ns.at[0], nr.at[0], s_next)
    ncp.start()
    ocp = []
    for k in (1, 2, 3):
        cp = remote(own.at[x], own.at[x], os.at[k - 1], orr.at[k - 1], at(x + k, z, y, c))
        cp.start()
        ocp.append(cp)

    for k in (1, 3, 2):
        ycp[k - 1].wait_recv()
        slot = lax.rem(y + 4 - k, 4) * 2 + c
        cp = remote(gath.at[slot], gath.at[slot], cs.at[k], cr.at[k], at(x, z, y, c + 1))
        cp.start()
        ccp.append(cp)
    ncp.wait_recv()
    n1cp = []
    for k in (1, 2, 3):
        cp = remote(n1.at[x], n1.at[x], n1s.at[k - 1], n1r.at[k - 1], at(x + k, z, y, c))
        cp.start()
        n1cp.append(cp)
    for cp in ccp:
        cp.wait_recv()
    zcp = []
    for k in (4, 3, 5, 2, 6, 1, 7):
        owner = (lax.rem(z + k, 8) * 4 + y) * 2 + c
        zsend[k - 1] = gath[lax.rem(ids[owner, 1], 8)]
        cp = remote(zsend.at[k - 1], zrecv.at[z], zs.at[k - 1], zr.at[k - 1], at(x, z + k, y, c))
        cp.start()
        zcp.append(cp)
    want = ids[s, 1]
    zrecv[z] = gath[lax.rem(want, 8)]
    for cp in zcp:
        cp.wait_recv()
    n2[x] = zrecv[lax.div(want, 8)]
    n2cp = []
    for k in (1, 2, 3):
        cp = remote(n2.at[x], n2.at[x], n2s.at[k - 1], n2r.at[k - 1], at(x + k, z, y, c))
        cp.start()
        n2cp.append(cp)
    for cp in ocp + n1cp + n2cp:
        cp.wait_recv()
    for cp in sums + ycp + ccp + [ncp] + ocp + n1cp + zcp + n2cp:
        cp.wait_send()


def comm_call(snap, basis, ids):
    vm = pl.BlockSpec(memory_space=pltpu.VMEM)
    dma = pltpu.SemaphoreType.DMA
    sems = [4, 3, 3, 3, 3, 3, 3, 4, 4, 1, 1, 3, 3, 7, 7, 3, 3]
    return pl.pallas_call(
        comm_kernel,
        out_shape=[jax.ShapeDtypeStruct((4, 64, 512), d) for d in (F32, BF, BF)],
        in_specs=[pl.BlockSpec(memory_space=pl.ANY), vm, pl.BlockSpec(memory_space=pltpu.SMEM)],
        out_specs=[vm] * 3,
        scratch_shapes=[pltpu.VMEM((512, 2048), BF), pltpu.VMEM((3, 64, 512), BF), pltpu.VMEM((3, 64, 512), BF),
                        pltpu.VMEM((8, 64, 512), BF), pltpu.VMEM((7, 64, 512), BF), pltpu.VMEM((8, 64, 512), BF)]
        + [dma((n,)) for n in sems],
        compiler_params=pltpu.CompilerParams(collective_id=0, has_side_effects=True, vmem_limit_bytes=40 * 2**20),
        name="exchange",
    )(snap, basis, ids)

RANK=64
PAD=8
TRI=[(i,j) for i in range(RANK) for j in range(i,RANK)]

def quad_tile(nf, c, q0, sub):
    out=None
    q=q0
    while q < q0+8:
        i,j=TRI[q]
        run=min(RANK-j, q0+8-q)
        b=q-q0
        val = nf[c, pl.ds(PAD+i,1), :] * nf[c, pl.ds(PAD+j-b, 8), :]
        out = val if out is None else jnp.where(sub < b, out, val)
        q+=run
    return out

def build_own(own, nf, F):
    T=2048
    e=None
    for r in range(4):
        v=own[r]; s=jnp.sum(v*v,axis=1,keepdims=True); e = s if e is None else e+s
    sc=lax.rsqrt(e/T+1e-6)
    for r in range(4):
        n=(own[r]*sc).astype(jnp.bfloat16)
        F[0:64, pl.ds(512*r,512)] = n
        nn=n.astype(jnp.float32)
        for k in range(4):
            nf[4*r+k, pl.ds(PAD,64), :] = nn[:, 128*k:128*k+128]

def build_nb(nb, row, F):
    T=2048
    e=None
    for r in range(4):
        v=nb[r].astype(jnp.float32); s=jnp.sum(v*v,axis=1,keepdims=True); e = s if e is None else e+s
    sc=lax.rsqrt(e/T+1e-6)
    for r in range(4):
        F[row:row+64, pl.ds(512*r,512)] = (nb[r].astype(jnp.float32)*sc).astype(jnp.bfloat16)

def build_quads(nf, F):
    sub=lax.broadcasted_iota(jnp.int32,(8,128),0)
    def chunk(c,_):
        col=pl.ds(pl.multiple_of(c*128,128),128)
        for t in range(0,len(TRI),16):
            a=quad_tile(nf,c,t,sub); b=quad_tile(nf,c,t+8,sub)
            F[192+t:192+t+16, col] = jnp.concatenate([a,b],0).astype(jnp.bfloat16)
        return 0
    lax.fori_loop(0,16,chunk,0)

def gram_kernel(own, n1, n2, o, F, nf, acc):
    j=pl.program_id(0)
    x=lax.axis_index("row")
    @pl.when(j==0)
    def _():
        nf[:, 0:PAD, :] = jnp.zeros((16,PAD,128),jnp.float32)
        nf[:, PAD+64:PAD+72, :] = jnp.zeros((16,8,128),jnp.float32)
        F[2272:2304,:]=jnp.zeros((32,2048),jnp.bfloat16)
        build_own(own,nf,F); build_nb(n1,64,F); build_nb(n2,128,F)
        build_quads(nf,F)
    rs=pl.multiple_of((x*568)//16*16,16)
    ofs=pl.multiple_of((x%2)*8,8)
    lhs=F[pl.ds(rs,576),:]
    rhs=F[pl.ds(pl.multiple_of(j*256,256),256),:]
    acc[...]=lax.dot_general(lhs,rhs,(((1,),(1,)),((),())),preferred_element_type=jnp.float32)
    o[...]=acc[pl.ds(ofs,568),:]*(1.0/2048)

def gram_call(own,n1,n2):
    return pl.pallas_call(gram_kernel, grid=(9,),
        out_shape=jax.ShapeDtypeStruct((568,2272),jnp.float32),
        in_specs=[pl.BlockSpec((4,64,512),lambda j:(0,0,0))]*3,
        out_specs=pl.BlockSpec((568,256),lambda j:(0,j)),
        scratch_shapes=[pltpu.VMEM((2304,2048),jnp.bfloat16), pltpu.VMEM((16,PAD+72,128),jnp.float32), pltpu.VMEM((576,256),jnp.float32)],
        compiler_params=pltpu.CompilerParams(vmem_limit_bytes=60*2**20, dimension_semantics=("arbitrary",)), name="gram")(own,n1,n2)


def on_device(snapshots, basis, neighbour_ids):
    own, n1, n2 = comm_call(snapshots[0], basis[0], neighbour_ids)
    return gram_call(own, n1, n2)[None]


def solution(mesh):
    return jax.shard_map(
        on_device,
        mesh=mesh,
        in_specs=(P("tm", "row", None), P("tm", "row", None), P()),
        out_specs=P("tm", "row", None),
        check_vma=False,
    )
```

time: 193 us -> 61.2 us (0.32); the launches traced: 191 us -> 61 us
  waiting for transfers between devices: 104 us -> 0 us
  Pallas kernels: 0 us -> 55.5 us
  blocking collectives: 20 us -> 0 us
  local copies, waits for them, and re-layouts: 24.5 us -> 5.5 us
  matrix products: 18.3 us -> 0 us
  between operations: 13.5 us -> 0.04 us
  other arithmetic: 9.68 us -> 0 us
    all_gather x1 -> x0, waiting for transfers between devices: 78.1 us -> none  [on_device(): every = lax.all_gather(normed[None], 'tm', axis=0, tiled=True)]
    pallas_call x0 -> x2, Pallas kernels: none -> 55.5 us  [the longest x1 41.8 us: comm_call(): pl.pallas_call(comm_kernel, out_shape=[jax.ShapeDtypeStruct((4, 64, 512),...]
    reduce_scatter x1 -> x0, waiting for transfers between devices: 26.2 us -> none  [on_device(): lax.psum_scatter(lax.dot_general(block, columns, (((0,), (0,)), ((), ()))...]
    dot_general x14 -> x0, matrix products: 18.3 us -> none  [the longest x4 9.34 us: add_block(): lax.dot_general(rows, feats, (((0,), (0,)), ((), ())), preferred_element_...]
    all_gather x1 -> x0, blocking collectives: 13.4 us -> none  [on_device(): piece = lax.all_gather(stacked, 'row', axis=1, tiled=True)]
    while x24 -> x0, local copies, waits for them, and re-layouts: 13.3 us -> none
    psum x1 -> x0, blocking collectives: 6.59 us -> none  [on_device(): energy = lax.psum(jnp.sum(local * local, axis=0), 'row')]
    broadcast_in_dim x2 -> x0, other arithmetic: 6.16 us -> none  [the longest x1 5.18 us: on_device(): return (carry / total_time)[None]]
  transfers between devices with their start and end apart: 2 -> 0, of which waited for: 2 -> 0; matrix products, arithmetic and copies ran while one was open for 1% -> 0% of each run, Pallas kernels for 0% -> 0%
where the time goes in v1:
time: 61.2 us; the launch traced here: 61 us
  Pallas kernels  55.5 us (91%)
  local copies, waits for them, and re-layouts  5.5 us (9%)
    pallas_call x1, Pallas kernels, comm_call(): pl.pallas_call(comm_kernel, out_shape=[jax.ShapeDtypeStruct((4, 64, 512),...  41.8 us
    pallas_call x1, Pallas kernels, gram_call(): pl.pallas_call(gram_kernel, grid=(9,), out_shape=jax.ShapeDtypeStruct((56...  13.7 us
    unnamed x10, local copies, waits for them, and re-layouts  5.5 us

profile of v1, /device:TPU:1, one launch (start us, length us, event | category | flops | bytes accessed | tf_op | source)
XLA Modules:
  0.0 61.0 jit_solution(16780981962357482518)
XLA Ops:
  0.0 0.8 %copy.5.ids = s32[64,2]{1,0:T(8,128)S(1)} copy(s32[64,2]{0,1:T(2,128)} %param.5) | data formatting | bytes 1024 | tf_op args[2]
  0.8 1.0 %copy.4 = bf16[1,512,64]{2,1,0:T(8,128)(2,1)S(1)} copy(bf16[1,512,64]{1,2,0:T(8,128)(2,1)} %param.4) | data formatting | bytes 131072 | tf_op args[1]
  1.7 0.0 copy-start
  1.7 1.6 %copy-done = bf16[1,512,2048]{2,1,0:T(8,128)(2,1)S(1)} copy-done((bf16[1,512,2048]{2,1,0:T(8,128)(2,1)S(1)}, bf16[1,512,2048]{2,1,0:T(8,128)(2,1)}, u32[]{:S(2)}) %copy-start) | copy-done | bytes 2097176
  3.3 41.8 %exchange.1 = (f32[4,64,512]{2,1,0:T(8,128)S(1)}, bf16[4,64,512]{2,1,0:T(8,128)(2,1)S(1)}, bf16[4,64,512]{2,1,0:T(8,128)(2,1)S(1)}) custom-call(bf16[512,2048]{1,0:T(8,128)(2,1)S(1)} %bitcast.3, bf16[512,64]{1,0:T(8,128)(2,1)S(1)} %bitcast.4, s32[64,2]{1,0:T(8,128)S(1)} %copy.5.ids), custom_call_target="tpu_custom_call" | custom-call | tf_op jit(solution)/shard_map/exchange/pallas_call | solution.py:125
  45.1 0.0 copy-start.1
  45.1 0.8 %copy-done.1 = f32[4,64,512]{2,1,0:T(8,128)} copy-done((f32[4,64,512]{2,1,0:T(8,128)}, f32[4,64,512]{2,1,0:T(8,128)S(1)}, u32[]{:S(2)}) %copy-start.1) | copy-done | bytes 524312
  45.9 0.0 copy-start.2
  45.9 0.7 %copy-done.2 = bf16[4,64,512]{2,1,0:T(8,128)(2,1)} copy-done((bf16[4,64,512]{2,1,0:T(8,128)(2,1)}, bf16[4,64,512]{2,1,0:T(8,128)(2,1)S(1)}, u32[]{:S(2)}) %copy-start.2) | copy-done | bytes 262168
  46.6 0.0 copy-start.3
  46.6 0.7 %copy-done.3 = bf16[4,64,512]{2,1,0:T(8,128)(2,1)} copy-done((bf16[4,64,512]{2,1,0:T(8,128)(2,1)}, bf16[4,64,512]{2,1,0:T(8,128)(2,1)S(1)}, u32[]{:S(2)}) %copy-start.3) | copy-done | bytes 262168
  47.3 13.7 %gram.1 = f32[568,2272]{1,0:T(8,128)} custom-call(f32[4,64,512]{2,1,0:T(8,128)} %copy-done.1, bf16[4,64,512]{2,1,0:T(8,128)(2,1)} %copy-done.2, bf16[4,64,512]{2,1,0:T(8,128)(2,1)} %copy-done.3), custom_call_target="tpu_custom_call" | custom-call | tf_op jit(solution)/shard_map/gram/pallas_call | solution.py:203
Async XLA Ops:
  1.7 1.6 %copy-start = (bf16[1,512,2048]{2,1,0:T(8,128)(2,1)S(1)}, bf16[1,512,2048]{2,1,0:T(8,128)(2,1)}, u32[]{:S(2)}) copy-start(bf16[1,512,2048]{2,1,0:T(8,128)(2,1)} %param.3) | copy-start | bytes 6291460
  45.1 0.8 %copy-start.1 = (f32[4,64,512]{2,1,0:T(8,128)}, f32[4,64,512]{2,1,0:T(8,128)S(1)}, u32[]{:S(2)}) copy-start(f32[4,64,512]{2,1,0:T(8,128)S(1)} %get-tuple-element.8.own) | copy-start | bytes 1572868
  45.9 0.7 %copy-start.2 = (bf16[4,64,512]{2,1,0:T(8,128)(2,1)}, bf16[4,64,512]{2,1,0:T(8,128)(2,1)S(1)}, u32[]{:S(2)}) copy-start(bf16[4,64,512]{2,1,0:T(8,128)(2,1)S(1)} %get-tuple-element.9.n1) | copy-start | bytes 786436
  46.6 0.7 %copy-start.3 = (bf16[4,64,512]{2,1,0:T(8,128)(2,1)}, bf16[4,64,512]{2,1,0:T(8,128)(2,1)S(1)}, u32[]{:S(2)}) copy-start(bf16[4,64,512]{2,1,0:T(8,128)(2,1)S(1)} %get-tuple-element.10.n2) | copy-start | bytes 786436

commit v2 on v1

v2 whole, which is shorter than its diff:
```python
import jax
import jax.numpy as jnp
import numpy as np
from jax import lax
from jax.experimental import pallas as pl
from jax.experimental.pallas import tpu as pltpu
from jax.sharding import PartitionSpec as P

MESH = pl.DeviceIdType.MESH
BF = jnp.bfloat16
F32 = jnp.float32
RANK = 64
TIME = 2048
EPS = 1e-6
PAIRS = [(i, j) for i in range(RANK) for j in range(i, RANK)]
ROWS = 568
COLS = 2272
PAD = 8
NT = (((1,), (1,)), ((), ()))


def place():
    t = lax.axis_index("tm")
    return lax.axis_index("row"), lax.div(t, 8), lax.rem(lax.div(t, 2), 4), lax.rem(t, 2)


def at(x, z, y, c):
    return (lax.rem(x, 4), (lax.rem(z, 8) * 4 + lax.rem(y, 4)) * 2 + lax.rem(c, 2))


def remote(src, dst, ss, rs, dev):
    return pltpu.make_async_remote_copy(
        src_ref=src, dst_ref=dst, send_sem=ss, recv_sem=rs, device_id=dev, device_id_type=MESH
    )


def scale_of(blocks):
    energy = None
    for v in blocks:
        e = jnp.sum(v * v, axis=1, keepdims=True)
        energy = e if energy is None else energy + e
    return lax.rsqrt(energy / TIME + EPS)


def quad_tile(nf, chunk, first, line):
    out, q = None, first
    while q < first + 8:
        i, j = PAIRS[q]
        b = q - first
        val = nf[chunk, pl.ds(PAD + i, 1), :] * nf[chunk, pl.ds(PAD + j - b, 8), :]
        out = val if out is None else jnp.where(line < b, out, val)
        q += min(RANK - j, first + 8 - q)
    return out


def build_quads(nf, feats):
    line = lax.broadcasted_iota(jnp.int32, (8, 128), 0)

    def one(chunk, carry):
        col = pl.ds(pl.multiple_of(chunk * 128, 128), 128)
        for t in range(0, len(PAIRS), 16):
            pair = [quad_tile(nf, chunk, t, line), quad_tile(nf, chunk, t + 8, line)]
            feats[192 + t : 208 + t, col] = jnp.concatenate(pair, 0).astype(BF)
        return carry

    lax.fori_loop(0, TIME // 128, one, 0)


def exchange(snap, basis, ids_hbm, feats, gram,
             sv, bv, ids, psend, precv, own, raw, nf, gy, gz, zsend, zrecv, mix, msend, ysend, yrecv, n1, n2,
             ld, ps, pr, os, orr, ys, yr, cs, cr, gs, gr, ns, nr, n1s, n1r, zs, zr, ms, mr, qs, qr, n2s, n2r):
    x, z, y, c = place()
    s = lax.axis_index("tm")
    me = y * 2 + c
    s_next = (x, lax.rem(s + 1, 64))
    s_prev = (x, lax.rem(s + 63, 64))

    def cols(q):
        return pl.ds(pl.multiple_of(q * 512, 512), 512)

    order = (2, 1, 3, 0)
    quarter = [lax.rem(x + k, 4) for k in order]
    fetch = [pltpu.make_async_copy(basis, bv, ld.at[4]), pltpu.make_async_copy(ids_hbm, ids, ld.at[5])]
    loads = [pltpu.make_async_copy(snap.at[:, cols(q)], sv.at[:, cols(q)], ld.at[i]) for i, q in enumerate(quarter)]
    fetch[0].start()
    for cp in loads:
        cp.start()
    fetch[1].start()

    bar = pltpu.get_barrier_semaphore()
    peers = [at(x + k, z, y, c) for k in (1, 2, 3)] + [at(x, z, y + k, c) for k in (1, 2, 3)]
    peers += [at(x, z + k, y, c) for k in range(1, 8)] + [at(x, z, y, c + 1), s_next, s_prev]
    for p in peers:
        pl.semaphore_signal(bar, inc=1, device_id=p, device_id_type=MESH)

    def project(i):
        loads[i].wait()
        return jnp.dot(bv[...], sv[:, cols(quarter[i])], preferred_element_type=F32)

    fetch[0].wait()
    sums = []
    for i, k in enumerate(order[:3]):
        psend[i] = project(i).astype(BF)
        if i == 0:
            pl.semaphore_wait(bar, len(peers))
        cp = remote(psend.at[i], precv.at[i], ps.at[i], pr.at[i], at(x + k, z, y, c))
        cp.start()
        sums.append(cp)
    total = project(3)
    fetch[1].wait()
    feats[128:192, :] = jnp.zeros((64, TIME), BF)
    feats[COLS:, :] = jnp.zeros((feats.shape[0] - COLS, TIME), BF)
    nf[:, 0:PAD, :] = jnp.zeros((16, PAD, 128), F32)
    nf[:, PAD + RANK :, :] = jnp.zeros((16, 8, 128), F32)
    for i in range(3):
        sums[i].wait_recv()
        total = total + precv[i].astype(F32)

    own[x] = total
    low = total.astype(BF)
    gy[me] = low[:, :256]
    gz[z] = low[:, 256:]
    raw[...] = low
    ycp = {}
    for k in (2, 1, 3):
        ycp[k] = remote(gy.at[me], gy.at[me], ys.at[k - 1], yr.at[k - 1], at(x, z, y + k, c))
        ycp[k].start()
    ccp = [remote(gy.at[me], gy.at[me], cs.at[0], cr.at[0], at(x, z, y, c + 1))]
    ccp[0].start()
    gcp = {}
    for k in (4, 3, 5, 2, 6, 1, 7):
        gcp[k] = remote(gz.at[z], gz.at[z], gs.at[k - 1], gr.at[k - 1], at(x, z + k, y, c))
        gcp[k].start()
    ncp = remote(raw, n1.at[x], ns.at[0], nr.at[0], s_next)
    ncp.start()
    ocp = []
    for k in (2, 1, 3):
        cp = remote(own.at[x], own.at[x], os.at[k - 1], orr.at[k - 1], at(x + k, z, y, c))
        cp.start()
        ocp.append(cp)

    for k in (1, 3, 2):
        ycp[k].wait_recv()
        slot = lax.rem(y + 4 - k, 4) * 2 + c
        cp = remote(gy.at[slot], gy.at[slot], cs.at[k], cr.at[k], at(x, z, y, c + 1))
        cp.start()
        ccp.append(cp)
    for cp in ccp:
        cp.wait_recv()
    want = ids[1, s]
    zcp = {}
    for k in (4, 3, 5, 2, 6, 1, 7):
        asked = ids[1, (lax.rem(z + k, 8) * 4 + y) * 2 + c]
        zsend[k - 1] = gy[lax.rem(asked, 8)]
        zcp[k] = remote(zsend.at[k - 1], zrecv.at[z], zs.at[k - 1], zr.at[k - 1], at(x, z + k, y, c))
        zcp[k].start()
    zrecv[z] = gy[lax.rem(want, 8)]

    ncp.wait_recv()
    n1cp = []
    for k in (2, 1, 3):
        cp = remote(n1.at[x], n1.at[x], n1s.at[k - 1], n1r.at[k - 1], at(x + k, z, y, c))
        cp.start()
        n1cp.append(cp)

    for k in (1, 7, 2, 6, 3, 5, 4):
        gcp[k].wait_recv()
    for yy in range(4):
        msend[yy] = gz[lax.div(ids[1, (z * 4 + yy) * 2 + 1 - c], 8)]
    mcp = remote(msend, mix.at[c], ms.at[0], mr.at[0], at(x, z, y, c + 1))
    mcp.start()
    for yy in range(4):
        mix[c, yy] = gz[lax.div(ids[1, (z * 4 + yy) * 2 + c], 8)]

    for cp in ocp:
        cp.wait_recv()
    scale = scale_of([own[r] for r in range(4)])
    for r in range(4):
        n = (own[r] * scale).astype(BF)
        feats[0:64, 512 * r : 512 * r + 512] = n
        wide = n.astype(F32)
        for k in range(4):
            nf[4 * r + k, pl.ds(PAD, RANK), :] = wide[:, 128 * k : 128 * k + 128]

    mcp.wait_recv()
    qcp = []
    for k in (2, 1, 3):
        yy = lax.rem(y + k, 4)
        asked = ids[1, (z * 4 + yy) * 2 + c]
        ysend[k - 1] = mix[lax.rem(asked, 2), yy]
        cp = remote(ysend.at[k - 1], yrecv.at[y], qs.at[k - 1], qr.at[k - 1], at(x, z, y + k, c))
        cp.start()
        qcp.append(cp)
    yrecv[y] = mix[lax.rem(want, 2), y]

    def neighbour(ref, row):
        blocks = [ref[r].astype(F32) for r in range(4)]
        scale = scale_of(blocks)
        for r in range(4):
            feats[row : row + 64, 512 * r : 512 * r + 512] = (blocks[r] * scale).astype(BF)

    for cp in n1cp:
        cp.wait_recv()
    neighbour(n1, 64)
    build_quads(nf, feats)

    n2cp = []

    def share(h):
        for k in (2, 1, 3):
            sem = 3 * h + k - 1
            cp = remote(n2.at[h, x], n2.at[h, x], n2s.at[sem], n2r.at[sem], at(x + k, z, y, c))
            cp.start()
            n2cp.append(cp)

    for cp in qcp:
        cp.wait_recv()
    n2[1, x] = yrecv[lax.div(lax.rem(want, 8), 2)]
    share(1)
    for k in (1, 7, 2, 6, 3, 5, 4):
        zcp[k].wait_recv()
    n2[0, x] = zrecv[lax.div(want, 8)]
    share(0)

    start = pl.multiple_of(lax.div(x * ROWS, 16) * 16, 16)
    lines = pl.ds(start, 576)
    for lo, hi in [(0, 128)] + [(k, min(k + 256, COLS)) for k in range(256, COLS, 256)]:
        top = min(lo + 256, feats.shape[0]) if lo else 128
        block = lax.dot_general(feats[lines, :], feats[lo:top, :], NT, preferred_element_type=F32)
        gram[:, lo:hi] = block[:, : hi - lo] * (1.0 / TIME)

    for cp in n2cp:
        cp.wait_recv()
    halves = [n2[h, r].astype(F32) for r in range(4) for h in range(2)]
    scale = scale_of(halves)
    for r in range(8):
        feats[128:192, 256 * r : 256 * r + 256] = (halves[r] * scale).astype(BF)
    for cp in sums + list(ycp.values()) + ccp + list(gcp.values()) + [ncp] + ocp + n1cp + list(zcp.values()) + [mcp] + qcp + n2cp:
        cp.wait_send()


def exchange_call(snap, basis, ids):
    vm = pl.BlockSpec(memory_space=pltpu.VMEM)
    hbm = pl.BlockSpec(memory_space=pltpu.HBM)
    dma = pltpu.SemaphoreType.DMA
    half = (64, 256)
    full = (64, 512)
    sems = [6, 3, 3, 3, 3, 3, 3, 4, 4, 7, 7, 1, 1, 3, 3, 7, 7, 1, 1, 3, 3, 6, 6]
    bufs = [(512, 2048), (64, 512), None, (3,) + full, (3,) + full, (4,) + full, full, (16, PAD + RANK + 8, 128),
            (8,) + half, (8,) + half, (7,) + half, (8,) + half, (2, 4) + half, (4,) + half, (3,) + half, (4,) + half,
            (4,) + full, (2, 4) + half]
    wide = (5, 7)
    scratch = [pltpu.SMEM((2, 64), jnp.int32) if b is None else pltpu.VMEM(b, F32 if i in wide else BF) for i, b in enumerate(bufs)]
    return pl.pallas_call(
        exchange,
        out_shape=[jax.ShapeDtypeStruct((2304, TIME), BF), jax.ShapeDtypeStruct((576, COLS), F32)],
        in_specs=[hbm] * 3,
        out_specs=[vm] * 2,
        scratch_shapes=scratch + [dma((n,)) for n in sems],
        compiler_params=pltpu.CompilerParams(collective_id=0, has_side_effects=True, vmem_limit_bytes=24 * 2**20),
        name="exchange",
    )(snap, basis, ids)


def finish(feats, gram, out, mid, rows, sem):
    x = lax.axis_index("row")
    off = pl.multiple_of(lax.rem(x, 2) * 8, 8)
    spans = [(0, 128), (256, COLS)]

    def ship(src, lo, hi, cl, ch, n):
        return pltpu.make_async_copy(src, out.at[pl.ds(lo, hi - lo), pl.ds(cl, ch - cl)], sem.at[n])

    early = []
    for n, (cl, ch) in enumerate(spans):
        for m, (lo, hi) in enumerate([(0, 128), (192, ROWS)]):
            early.append(ship(gram.at[pl.ds(off + lo, hi - lo), pl.ds(cl, ch - cl)], lo, hi, cl, ch, 2 * n + m))
    for cp in early:
        cp.start()
    middle = [ship(gram.at[pl.ds(off + 128, 64), pl.ds(cl, ch - cl)], 128, 192, cl, ch, 4 + n) for n, (cl, ch) in enumerate(spans)]
    late = [ship(rows.at[:, pl.ds(cl, ch - cl)], 128, 192, cl, ch, 4 + n) for n, (cl, ch) in enumerate(spans)]

    @pl.when(x != 0)
    def _():
        for cp in middle:
            cp.start()

    lines = pl.ds(pl.multiple_of(lax.div(x * ROWS, 16) * 16, 16), 576)
    mid[...] = lax.dot_general(feats[lines, :], feats[128:256, :], NT, preferred_element_type=F32) * (1.0 / TIME)
    centre = ship(mid.at[pl.ds(off, ROWS), :], 0, ROWS, 128, 256, 6)
    centre.start()

    @pl.when(x == 0)
    def _():
        for lo in range(0, COLS, 256):
            hi = min(lo + 256, COLS)
            block = lax.dot_general(feats[128:192, :], feats[lo : lo + 256, :], NT, preferred_element_type=F32)
            rows[:, lo:hi] = block[:, : hi - lo] * (1.0 / TIME)
        for cp in late:
            cp.start()

    for cp in early + middle + [centre]:
        cp.wait()


def finish_call(feats, gram):
    vm = pl.BlockSpec(memory_space=pltpu.VMEM)
    return pl.pallas_call(
        finish,
        out_shape=jax.ShapeDtypeStruct((ROWS, COLS), F32),
        in_specs=[vm] * 2,
        out_specs=pl.BlockSpec(memory_space=pltpu.HBM),
        scratch_shapes=[pltpu.VMEM((576, 128), F32), pltpu.VMEM((64, COLS), F32), pltpu.SemaphoreType.DMA((7,))],
        compiler_params=pltpu.CompilerParams(vmem_limit_bytes=8 * 2**20),
        name="finish",
    )(feats, gram)


def on_device(snapshots, basis, neighbour_ids):
    feats, gram = exchange_call(snapshots[0], basis[0].T, neighbour_ids.T)
    return finish_call(feats, gram)[None]


def solution(mesh):
    return jax.shard_map(
        on_device,
        mesh=mesh,
        in_specs=(P("tm", "row", None), P("tm", "row", None), P()),
        out_specs=P("tm", "row", None),
        check_vma=False,
    )
```

time: 61.2 us -> 46.1 us (0.75)
  Pallas kernels: 55.5 us -> 42.8 us
  local copies, waits for them, and re-layouts: 5.5 us -> 3.11 us
    pallas_call x2, Pallas kernels: 55.5 us -> 42.8 us  [the longest x1 38.2 us: exchange_call(): pl.pallas_call(exchange, out_shape=[jax.ShapeDtypeStruct((2304, TIME), BF...]
    unnamed x10 -> x6, local copies, waits for them, and re-layouts: 5.5 us -> 3.11 us
where the time goes in v2:
time: 46.1 us; the launch traced here: 45.9 us
  Pallas kernels  42.8 us (93%)
  local copies, waits for them, and re-layouts  3.11 us (7%)
    pallas_call x1, Pallas kernels, exchange_call(): pl.pallas_call(exchange, out_shape=[jax.ShapeDtypeStruct((2304, TIME), BF...  38.2 us
    pallas_call x1, Pallas kernels, finish_call(): pl.pallas_call(finish, out_shape=jax.ShapeDtypeStruct((ROWS, COLS), F32),...  4.59 us
    unnamed x6, local copies, waits for them, and re-layouts  3.11 us

profile of v2, /device:TPU:1, one launch (start us, length us, event | category | flops | bytes accessed | tf_op | source)
XLA Modules:
  0.0 45.9 jit_solution(13364378503973092271)
XLA Ops:
  0.0 0.0 copy-start
  0.0 1.6 %copy-done = bf16[1,512,2048]{2,1,0:T(8,128)(2,1)S(1)} copy-done((bf16[1,512,2048]{2,1,0:T(8,128)(2,1)S(1)}, bf16[1,512,2048]{2,1,0:T(8,128)(2,1)}, u32[]{:S(2)}) %copy-start) | copy-done | bytes 2097176
  1.6 0.0 copy-start.1
  1.6 0.8 %copy-done.1 = bf16[1,512,64]{1,2,0:T(8,128)(2,1)S(1)} copy-done((bf16[1,512,64]{1,2,0:T(8,128)(2,1)S(1)}, bf16[1,512,64]{1,2,0:T(8,128)(2,1)}, u32[]{:S(2)}) %copy-start.1) | copy-done | bytes 65560
  2.4 0.0 copy-start.2
  2.4 0.7 %copy-done.2 = s32[64,2]{0,1:T(2,128)S(1)} copy-done((s32[64,2]{0,1:T(2,128)S(1)}, s32[64,2]{0,1:T(2,128)}, u32[]{:S(2)}) %copy-start.2) | copy-done | bytes 536
  3.1 38.2 %exchange.1 = (bf16[2304,2048]{1,0:T(8,128)(2,1)S(1)}, f32[576,2272]{1,0:T(8,128)S(1)}) custom-call(bf16[512,2048]{1,0:T(8,128)(2,1)S(1)} %bitcast.6, bf16[64,512]{1,0:T(8,128)(2,1)S(1)} %bitcast.7, s32[2,64]{1,0:T(2,128)S(1)} %bitcast.8), custom_call_target="tpu_custom_call" | custom-call | tf_op jit(solution)/shard_map/exchange/pallas_call | solution.py:254
  41.3 4.6 %finish.1 = f32[568,2272]{1,0:T(8,128)} custom-call(bf16[2304,2048]{1,0:T(8,128)(2,1)S(1)} %get-tuple-element.7.feats, f32[576,2272]{1,0:T(8,128)S(1)} %get-tuple-element.8.gram), custom_call_target="tpu_custom_call" | custom-call | tf_op jit(solution)/shard_map/finish/pallas_call | solution.py:307
Async XLA Ops:
  0.0 1.6 %copy-start = (bf16[1,512,2048]{2,1,0:T(8,128)(2,1)S(1)}, bf16[1,512,2048]{2,1,0:T(8,128)(2,1)}, u32[]{:S(2)}) copy-start(bf16[1,512,2048]{2,1,0:T(8,128)(2,1)} %param.3) | copy-start | bytes 6291460
  1.6 0.8 %copy-start.1 = (bf16[1,512,64]{1,2,0:T(8,128)(2,1)S(1)}, bf16[1,512,64]{1,2,0:T(8,128)(2,1)}, u32[]{:S(2)}) copy-start(bf16[1,512,64]{1,2,0:T(8,128)(2,1)} %param.4) | copy-start | bytes 196612
  2.4 0.7 %copy-start.2 = (s32[64,2]{0,1:T(2,128)S(1)}, s32[64,2]{0,1:T(2,128)}, u32[]{:S(2)}) copy-start(s32[64,2]{0,1:T(2,128)} %param.5) | copy-start | bytes 1540

commit v3 on v2

--- a/solution.py
+++ b/solution.py
@@ -16,6 +16,7 @@
 ROWS = 568
 COLS = 2272
 PAD = 8
+HEAD = 256
 NT = (((1,), (1,)), ((), ()))
 
 
@@ -53,7 +54,7 @@
     return out
 
 
-def build_quads(nf, feats):
+def build_quads(nf, feats, first, last):
     line = lax.broadcasted_iota(jnp.int32, (8, 128), 0)
 
     def one(chunk, carry):
@@ -63,7 +64,7 @@
             feats[192 + t : 208 + t, col] = jnp.concatenate(pair, 0).astype(BF)
         return carry
 
-    lax.fori_loop(0, TIME // 128, one, 0)
+    lax.fori_loop(first, last, one, 0)
 
 
 def exchange(snap, basis, ids_hbm, feats, gram,
@@ -108,7 +109,7 @@
         sums.append(cp)
     total = project(3)
     fetch[1].wait()
-    feats[128:192, :] = jnp.zeros((64, TIME), BF)
+    feats[64:192, :] = jnp.zeros((128, TIME), BF)
     feats[COLS:, :] = jnp.zeros((feats.shape[0] - COLS, TIME), BF)
     nf[:, 0:PAD, :] = jnp.zeros((16, PAD, 128), F32)
     nf[:, PAD + RANK :, :] = jnp.zeros((16, 8, 128), F32)
@@ -156,12 +157,30 @@
         zcp[k].start()
     zrecv[z] = gy[lax.rem(want, 8)]
 
-    ncp.wait_recv()
-    n1cp = []
-    for k in (2, 1, 3):
-        cp = remote(n1.at[x], n1.at[x], n1s.at[k - 1], n1r.at[k - 1], at(x + k, z, y, c))
-        cp.start()
-        n1cp.append(cp)
+    for cp in ocp:
+        cp.wait_recv()
+    scale = scale_of([own[r] for r in range(4)])
+    for r in range(4):
+        n = (own[r] * scale).astype(BF)
+        feats[0:64, 512 * r : 512 * r + 512] = n
+        wide = n.astype(F32)
+        for k in range(4):
+            nf[4 * r + k, pl.ds(PAD, RANK), :] = wide[:, 128 * k : 128 * k + 128]
+
+    def neighbour(ref, row):
+        blocks = [ref[r].astype(F32) for r in range(4)]
+        scale = scale_of(blocks)
+        for r in range(4):
+            feats[row : row + 64, 512 * r : 512 * r + 512] = (blocks[r] * scale).astype(BF)
+
+
+    lines = pl.ds(pl.multiple_of(lax.div(x * ROWS, 16) * 16, 16), 576)
+    spans = [(k, min(k + 256, COLS)) for k in range(HEAD, COLS, 256)]
+
+    def multiply(first, last):
+        for lo, hi in spans[first:last]:
+            block = lax.dot_general(feats[lines, :], feats[lo : lo + 256, :], NT, preferred_element_type=F32)
+            gram[:, lo - HEAD : hi - HEAD] = block[:, : hi - lo] * (1.0 / TIME)
 
     for k in (1, 7, 2, 6, 3, 5, 4):
         gcp[k].wait_recv()
@@ -172,15 +191,13 @@
     for yy in range(4):
         mix[c, yy] = gz[lax.div(ids[1, (z * 4 + yy) * 2 + c], 8)]
 
-    for cp in ocp:
-        cp.wait_recv()
-    scale = scale_of([own[r] for r in range(4)])
-    for r in range(4):
-        n = (own[r] * scale).astype(BF)
-        feats[0:64, 512 * r : 512 * r + 512] = n
-        wide = n.astype(F32)
-        for k in range(4):
-            nf[4 * r + k, pl.ds(PAD, RANK), :] = wide[:, 128 * k : 128 * k + 128]
+    ncp.wait_recv()
+    n1cp = []
+    for k in (2, 1, 3):
+        cp = remote(n1.at[x], n1.at[x], n1s.at[k - 1], n1r.at[k - 1], at(x + k, z, y, c))
+        cp.start()
+        n1cp.append(cp)
+    build_quads(nf, feats, 0, 6)
 
     mcp.wait_recv()
     qcp = []
@@ -193,17 +210,7 @@
         qcp.append(cp)
     yrecv[y] = mix[lax.rem(want, 2), y]
 
-    def neighbour(ref, row):
-        blocks = [ref[r].astype(F32) for r in range(4)]
-        scale = scale_of(blocks)
-        for r in range(4):
-            feats[row : row + 64, 512 * r : 512 * r + 512] = (blocks[r] * scale).astype(BF)
-
-    for cp in n1cp:
-        cp.wait_recv()
-    neighbour(n1, 64)
-    build_quads(nf, feats)
-
+    build_quads(nf, feats, 6, 16)
     n2cp = []
 
     def share(h):
@@ -222,13 +229,11 @@
     n2[0, x] = zrecv[lax.div(want, 8)]
     share(0)
 
-    start = pl.multiple_of(lax.div(x * ROWS, 16) * 16, 16)
-    lines = pl.ds(start, 576)
-    for lo, hi in [(0, 128)] + [(k, min(k + 256, COLS)) for k in range(256, COLS, 256)]:
-        top = min(lo + 256, feats.shape[0]) if lo else 128
-        block = lax.dot_general(feats[lines, :], feats[lo:top, :], NT, preferred_element_type=F32)
-        gram[:, lo:hi] = block[:, : hi - lo] * (1.0 / TIME)
-
+    multiply(0, 8)
+
+    for cp in n1cp:
+        cp.wait_recv()
+    neighbour(n1, 64)
     for cp in n2cp:
         cp.wait_recv()
     halves = [n2[h, r].astype(F32) for r in range(4) for h in range(2)]
@@ -253,7 +258,7 @@
     scratch = [pltpu.SMEM((2, 64), jnp.int32) if b is None else pltpu.VMEM(b, F32 if i in wide else BF) for i, b in enumerate(bufs)]
     return pl.pallas_call(
         exchange,
-        out_shape=[jax.ShapeDtypeStruct((2304, TIME), BF), jax.ShapeDtypeStruct((576, COLS), F32)],
+        out_shape=[jax.ShapeDtypeStruct((2304, TIME), BF), jax.ShapeDtypeStruct((576, COLS - HEAD), F32)],
         in_specs=[hbm] * 3,
         out_specs=[vm] * 2,
         scratch_shapes=scratch + [dma((n,)) for n in sems],
@@ -262,43 +267,37 @@
     )(snap, basis, ids)
 
 
-def finish(feats, gram, out, mid, rows, sem):
+def finish(feats, gram, out, head, band, sem):
     x = lax.axis_index("row")
     off = pl.multiple_of(lax.rem(x, 2) * 8, 8)
-    spans = [(0, 128), (256, COLS)]
-
-    def ship(src, lo, hi, cl, ch, n):
-        return pltpu.make_async_copy(src, out.at[pl.ds(lo, hi - lo), pl.ds(cl, ch - cl)], sem.at[n])
-
-    early = []
-    for n, (cl, ch) in enumerate(spans):
-        for m, (lo, hi) in enumerate([(0, 128), (192, ROWS)]):
-            early.append(ship(gram.at[pl.ds(off + lo, hi - lo), pl.ds(cl, ch - cl)], lo, hi, cl, ch, 2 * n + m))
+
+    def ship(src, lo, size, n):
+        return pltpu.make_async_copy(src, out.at[pl.ds(lo, size), pl.ds(HEAD, COLS - HEAD)], sem.at[n])
+
+    early = [ship(gram.at[pl.ds(off + lo, size), :], lo, size, n) for n, (lo, size) in enumerate([(192, 184), (376, 192), (0, 64)])]
+    middle = ship(gram.at[pl.ds(off + 64, 128), :], 64, 128, 3)
+    late = ship(band, 64, 128, 3)
     for cp in early:
         cp.start()
-    middle = [ship(gram.at[pl.ds(off + 128, 64), pl.ds(cl, ch - cl)], 128, 192, cl, ch, 4 + n) for n, (cl, ch) in enumerate(spans)]
-    late = [ship(rows.at[:, pl.ds(cl, ch - cl)], 128, 192, cl, ch, 4 + n) for n, (cl, ch) in enumerate(spans)]
 
     @pl.when(x != 0)
     def _():
-        for cp in middle:
-            cp.start()
+        middle.start()
 
     lines = pl.ds(pl.multiple_of(lax.div(x * ROWS, 16) * 16, 16), 576)
-    mid[...] = lax.dot_general(feats[lines, :], feats[128:256, :], NT, preferred_element_type=F32) * (1.0 / TIME)
-    centre = ship(mid.at[pl.ds(off, ROWS), :], 0, ROWS, 128, 256, 6)
-    centre.start()
+    head[...] = lax.dot_general(feats[lines, :], feats[0:HEAD, :], NT, preferred_element_type=F32) * (1.0 / TIME)
+    first = pltpu.make_async_copy(head.at[pl.ds(off, ROWS), :], out.at[:, pl.ds(0, HEAD)], sem.at[4])
+    first.start()
 
     @pl.when(x == 0)
     def _():
-        for lo in range(0, COLS, 256):
-            hi = min(lo + 256, COLS)
-            block = lax.dot_general(feats[128:192, :], feats[lo : lo + 256, :], NT, preferred_element_type=F32)
-            rows[:, lo:hi] = block[:, : hi - lo] * (1.0 / TIME)
-        for cp in late:
-            cp.start()
-
-    for cp in early + middle + [centre]:
+        for lo in range(HEAD, COLS, 768):
+            hi = min(lo + 768, COLS)
+            block = lax.dot_general(feats[64:192, :], feats[lo : lo + 768, :], NT, preferred_element_type=F32)
+            band[:, lo - HEAD : hi - HEAD] = block[:, : hi - lo] * (1.0 / TIME)
+        late.start()
+
+    for cp in early + [middle, first]:
         cp.wait()
 
 
@@ -309,14 +308,15 @@
         out_shape=jax.ShapeDtypeStruct((ROWS, COLS), F32),
         in_specs=[vm] * 2,
         out_specs=pl.BlockSpec(memory_space=pltpu.HBM),
-        scratch_shapes=[pltpu.VMEM((576, 128), F32), pltpu.VMEM((64, COLS), F32), pltpu.SemaphoreType.DMA((7,))],
+        scratch_shapes=[pltpu.VMEM((576, HEAD), F32), pltpu.VMEM((128, COLS - HEAD), F32), pltpu.SemaphoreType.DMA((5,))],
         compiler_params=pltpu.CompilerParams(vmem_limit_bytes=8 * 2**20),
         name="finish",
     )(feats, gram)
 
 
 def on_device(snapshots, basis, neighbour_ids):
-    feats, gram = exchange_call(snapshots[0], basis[0].T, neighbour_ids.T)
+    operands = [pltpu.with_memory_space_constraint(a, pltpu.HBM) for a in (snapshots[0], basis[0].T, neighbour_ids.T)]
+    feats, gram = exchange_call(*operands)
     return finish_call(feats, gram)[None]
 
 

time: 46.1 us -> 40.1 us (0.87)
  local copies, waits for them, and re-layouts: 3.11 us -> 0 us
  Pallas kernels: 42.8 us -> 39.7 us
    pallas_call x1, Pallas kernels: 38.2 us -> 35 us  [exchange_call(): pl.pallas_call(exchange, out_shape=[jax.ShapeDtypeStruct((2304, TIME), BF...]
    unnamed x6 -> x0, local copies, waits for them, and re-layouts: 3.11 us -> none
where the time goes in v3:
time: 40.1 us; the launch traced here: 39.7 us
  Pallas kernels  39.7 us (99%)
    pallas_call x1, Pallas kernels, exchange_call(): pl.pallas_call(exchange, out_shape=[jax.ShapeDtypeStruct((2304, TIME), BF...  35 us
    pallas_call x1, Pallas kernels, finish_call(): pl.pallas_call(finish, out_shape=jax.ShapeDtypeStruct((ROWS, COLS), F32),...  4.7 us

profile of v3, /device:TPU:1, one launch (start us, length us, event | category | flops | bytes accessed | tf_op | source)
XLA Modules:
  0.0 39.7 jit_solution(16441685564989264980)
XLA Ops:
  0.0 35.0 %exchange.1 = (bf16[2304,2048]{1,0:T(8,128)(2,1)S(1)}, f32[576,2016]{1,0:T(8,128)S(1)}) custom-call(bf16[512,2048]{1,0:T(8,128)(2,1)} %bitcast.6, bf16[64,512]{1,0:T(8,128)(2,1)} %bitcast.7, s32[2,64]{1,0:T(2,128)} %bitcast.8), custom_call_target="tpu_custom_call" | custom-call | tf_op jit(solution)/shard_map/exchange/pallas_call | solution.py:259
  35.0 4.7 %finish.1 = f32[568,2272]{1,0:T(8,128)} custom-call(bf16[2304,2048]{1,0:T(8,128)(2,1)S(1)} %get-tuple-element.7.feats, f32[576,2016]{1,0:T(8,128)S(1)} %get-tuple-element.8.gram), custom_call_target="tpu_custom_call" | custom-call | tf_op jit(solution)/shard_map/finish/pallas_call | solution.py:306

commit v4 on v3

--- a/solution.py
+++ b/solution.py
@@ -99,51 +99,56 @@
         return jnp.dot(bv[...], sv[:, cols(quarter[i])], preferred_element_type=F32)
 
     fetch[0].wait()
-    sums = []
-    for i, k in enumerate(order[:3]):
+    sums = {}
+
+    def give(i, h):
+        part = pl.ds(256 * h, 256)
+        sums[i, h] = remote(psend.at[i, :, part], precv.at[i, :, part], ps.at[2 * i + h], pr.at[2 * i + h], at(x + order[i], z, y, c))
+        sums[i, h].start()
+
+    for i in range(3):
         psend[i] = project(i).astype(BF)
         if i == 0:
             pl.semaphore_wait(bar, len(peers))
-        cp = remote(psend.at[i], precv.at[i], ps.at[i], pr.at[i], at(x + k, z, y, c))
-        cp.start()
-        sums.append(cp)
+        give(i, 0)
+    for i in range(3):
+        give(i, 1)
     total = project(3)
     fetch[1].wait()
     feats[64:192, :] = jnp.zeros((128, TIME), BF)
     feats[COLS:, :] = jnp.zeros((feats.shape[0] - COLS, TIME), BF)
     nf[:, 0:PAD, :] = jnp.zeros((16, PAD, 128), F32)
     nf[:, PAD + RANK :, :] = jnp.zeros((16, 8, 128), F32)
+    lower = total[:, :256]
     for i in range(3):
-        sums[i].wait_recv()
-        total = total + precv[i].astype(F32)
-
-    own[x] = total
-    low = total.astype(BF)
-    gy[me] = low[:, :256]
-    gz[z] = low[:, 256:]
-    raw[...] = low
-    ycp = {}
-    for k in (2, 1, 3):
-        ycp[k] = remote(gy.at[me], gy.at[me], ys.at[k - 1], yr.at[k - 1], at(x, z, y + k, c))
-        ycp[k].start()
-    ccp = [remote(gy.at[me], gy.at[me], cs.at[0], cr.at[0], at(x, z, y, c + 1))]
-    ccp[0].start()
-    gcp = {}
-    for k in (4, 3, 5, 2, 6, 1, 7):
-        gcp[k] = remote(gz.at[z], gz.at[z], gs.at[k - 1], gr.at[k - 1], at(x, z + k, y, c))
-        gcp[k].start()
+        sums[i, 0].wait_recv()
+        lower = lower + precv[i, :, :256].astype(F32)
+    gy[me] = lower.astype(BF)
+    ycp = [remote(gy.at[me], gy.at[me], ys.at[i], yr.at[i], at(x, z, y + k, c)) for i, k in enumerate((2, 1, 3))]
+    ccp = [remote(gy.at[me], gy.at[me], cs.at[3], cr.at[3], at(x, z, y, c + 1))]
+    for cp in ycp + ccp:
+        cp.start()
+    upper = total[:, 256:]
+    for i in range(3):
+        sums[i, 1].wait_recv()
+        upper = upper + precv[i, :, 256:].astype(F32)
+    gz[z] = upper.astype(BF)
+    gcp = [remote(gz.at[z], gz.at[z], gs.at[k - 1], gr.at[k - 1], at(x, z + k, y, c)) for k in (4, 3, 5, 2, 6, 1, 7)]
+    for cp in gcp:
+        cp.start()
+    own[x, :, :256] = lower
+    own[x, :, 256:] = upper
+    raw[:, :256] = lower.astype(BF)
+    raw[:, 256:] = upper.astype(BF)
     ncp = remote(raw, n1.at[x], ns.at[0], nr.at[0], s_next)
-    ncp.start()
-    ocp = []
-    for k in (2, 1, 3):
-        cp = remote(own.at[x], own.at[x], os.at[k - 1], orr.at[k - 1], at(x + k, z, y, c))
-        cp.start()
-        ocp.append(cp)
-
-    for k in (1, 3, 2):
-        ycp[k].wait_recv()
+    ocp = [remote(own.at[x], own.at[x], os.at[i], orr.at[i], at(x + k, z, y, c)) for i, k in enumerate((2, 1, 3))]
+    for cp in ocp + [ncp]:
+        cp.start()
+
+    for i, k in ((1, 1), (2, 3), (0, 2)):
+        ycp[i].wait_recv()
         slot = lax.rem(y + 4 - k, 4) * 2 + c
-        cp = remote(gy.at[slot], gy.at[slot], cs.at[k], cr.at[k], at(x, z, y, c + 1))
+        cp = remote(gy.at[slot], gy.at[slot], cs.at[i], cr.at[i], at(x, z, y, c + 1))
         cp.start()
         ccp.append(cp)
     for cp in ccp:
@@ -178,12 +183,22 @@
     spans = [(k, min(k + 256, COLS)) for k in range(HEAD, COLS, 256)]
 
     def multiply(first, last):
-        for lo, hi in spans[first:last]:
-            block = lax.dot_general(feats[lines, :], feats[lo : lo + 256, :], NT, preferred_element_type=F32)
-            gram[:, lo - HEAD : hi - HEAD] = block[:, : hi - lo] * (1.0 / TIME)
-
-    for k in (1, 7, 2, 6, 3, 5, 4):
-        gcp[k].wait_recv()
+        @pl.when(x == 0)
+        def _():
+            for lo, hi in spans[first:last]:
+                left = jnp.concatenate([feats[0:64, :], feats[192:576, :]], 0)
+                block = lax.dot_general(left, feats[lo : lo + 256, :], NT, preferred_element_type=F32)[:, : hi - lo] * (1.0 / TIME)
+                gram[0:64, lo - HEAD : hi - HEAD] = block[0:64]
+                gram[192:576, lo - HEAD : hi - HEAD] = block[64:]
+
+        @pl.when(x != 0)
+        def _():
+            for lo, hi in spans[first:last]:
+                block = lax.dot_general(feats[lines, :], feats[lo : lo + 256, :], NT, preferred_element_type=F32)
+                gram[:, lo - HEAD : hi - HEAD] = block[:, : hi - lo] * (1.0 / TIME)
+
+    for cp in gcp:
+        cp.wait_recv()
     for yy in range(4):
         msend[yy] = gz[lax.div(ids[1, (z * 4 + yy) * 2 + 1 - c], 8)]
     mcp = remote(msend, mix.at[c], ms.at[0], mr.at[0], at(x, z, y, c + 1))
@@ -240,7 +255,7 @@
     scale = scale_of(halves)
     for r in range(8):
         feats[128:192, 256 * r : 256 * r + 256] = (halves[r] * scale).astype(BF)
-    for cp in sums + list(ycp.values()) + ccp + list(gcp.values()) + [ncp] + ocp + n1cp + list(zcp.values()) + [mcp] + qcp + n2cp:
+    for cp in list(sums.values()) + ycp + ccp + gcp + [ncp] + ocp + n1cp + list(zcp.values()) + [mcp] + qcp + n2cp:
         cp.wait_send()
 
 
@@ -250,7 +265,7 @@
     dma = pltpu.SemaphoreType.DMA
     half = (64, 256)
     full = (64, 512)
-    sems = [6, 3, 3, 3, 3, 3, 3, 4, 4, 7, 7, 1, 1, 3, 3, 7, 7, 1, 1, 3, 3, 6, 6]
+    sems = [6, 6, 6, 3, 3, 3, 3, 4, 4, 7, 7, 1, 1, 3, 3, 7, 7, 1, 1, 3, 3, 6, 6]
     bufs = [(512, 2048), (64, 512), None, (3,) + full, (3,) + full, (4,) + full, full, (16, PAD + RANK + 8, 128),
             (8,) + half, (8,) + half, (7,) + half, (8,) + half, (2, 4) + half, (4,) + half, (3,) + half, (4,) + half,
             (4,) + full, (2, 4) + half]
@@ -276,7 +291,6 @@
 
     early = [ship(gram.at[pl.ds(off + lo, size), :], lo, size, n) for n, (lo, size) in enumerate([(192, 184), (376, 192), (0, 64)])]
     middle = ship(gram.at[pl.ds(off + 64, 128), :], 64, 128, 3)
-    late = ship(band, 64, 128, 3)
     for cp in early:
         cp.start()
 
@@ -289,16 +303,30 @@
     first = pltpu.make_async_copy(head.at[pl.ds(off, ROWS), :], out.at[:, pl.ds(0, HEAD)], sem.at[4])
     first.start()
 
+    late = []
+    for n, lo in enumerate(range(HEAD, COLS, 768)):
+        size = min(768, COLS - lo)
+        late.append(pltpu.make_async_copy(band.at[:, pl.ds(lo - HEAD, size)], out.at[pl.ds(64, 128), pl.ds(lo, size)], sem.at[5 + n]))
+
     @pl.when(x == 0)
     def _():
-        for lo in range(HEAD, COLS, 768):
+        for cp, lo in zip(late, range(HEAD, COLS, 768)):
             hi = min(lo + 768, COLS)
             block = lax.dot_general(feats[64:192, :], feats[lo : lo + 768, :], NT, preferred_element_type=F32)
             band[:, lo - HEAD : hi - HEAD] = block[:, : hi - lo] * (1.0 / TIME)
-        late.start()
-
-    for cp in early + [middle, first]:
+            cp.start()
+
+    for cp in early + [first]:
         cp.wait()
+
+    @pl.when(x != 0)
+    def _():
+        middle.wait()
+
+    @pl.when(x == 0)
+    def _():
+        for cp in late:
+            cp.wait()
 
 
 def finish_call(feats, gram):
@@ -308,7 +336,7 @@
         out_shape=jax.ShapeDtypeStruct((ROWS, COLS), F32),
         in_specs=[vm] * 2,
         out_specs=pl.BlockSpec(memory_space=pltpu.HBM),
-        scratch_shapes=[pltpu.VMEM((576, HEAD), F32), pltpu.VMEM((128, COLS - HEAD), F32), pltpu.SemaphoreType.DMA((5,))],
+        scratch_shapes=[pltpu.VMEM((576, HEAD), F32), pltpu.VMEM((128, COLS - HEAD), F32), pltpu.SemaphoreType.DMA((8,))],
         compiler_params=pltpu.CompilerParams(vmem_limit_bytes=8 * 2**20),
         name="finish",
     )(feats, gram)

time: 40.1 us -> 38.5 us (0.960)
  Pallas kernels: 39.7 us -> 38.4 us
    pallas_call x1, Pallas kernels: 35 us -> 34 us  [exchange_call(): pl.pallas_call(exchange, out_shape=[jax.ShapeDtypeStruct((2304, TIME), BF...]
where the time goes in v4:
time: 38.5 us; the launch traced here: 38.4 us
  Pallas kernels  38.4 us (100%)
    pallas_call x1, Pallas kernels, exchange_call(): pl.pallas_call(exchange, out_shape=[jax.ShapeDtypeStruct((2304, TIME), BF...  34 us
    pallas_call x1, Pallas kernels, finish_call(): pl.pallas_call(finish, out_shape=jax.ShapeDtypeStruct((ROWS, COLS), F32),...  4.44 us

profile of v4, /device:TPU:1, one launch (start us, length us, event | category | flops | bytes accessed | tf_op | source)
XLA Modules:
  0.0 38.4 jit_solution(12113496233083718925)
XLA Ops:
  0.0 34.0 %exchange.1 = (bf16[2304,2048]{1,0:T(8,128)(2,1)S(1)}, f32[576,2016]{1,0:T(8,128)S(1)}) custom-call(bf16[512,2048]{1,0:T(8,128)(2,1)} %bitcast.6, bf16[64,512]{1,0:T(8,128)(2,1)} %bitcast.7, s32[2,64]{1,0:T(2,128)} %bitcast.8), custom_call_target="tpu_custom_call" | custom-call | tf_op jit(solution)/shard_map/exchange/pallas_call | solution.py:274
  34.0 4.4 %finish.1 = f32[568,2272]{1,0:T(8,128)} custom-call(bf16[2304,2048]{1,0:T(8,128)(2,1)S(1)} %get-tuple-element.7.feats, f32[576,2016]{1,0:T(8,128)S(1)} %get-tuple-element.8.gram), custom_call_target="tpu_custom_call" | custom-call | tf_op jit(solution)/shard_map/finish/pallas_call | solution.py:334
